TPU v7x, 32 devices: a whole 2x2x4 slice. The times are simulated.
32 devices in a mesh: grid: 8 (over z, x), cols: 4 (over y, core).
Axes of the slice: x: 2, y: 2, z: 4, core: 2. Of those that a mesh axis runs over, the one named last changes fastest.
Arguments:
- basis: float32 [1024, 3, 16, 1024], P('cols', None, 'grid'), may hold values from -1 to 1
- snapshots: float32 [128, 3, 16, 1024], P('cols', None, 'grid'), may hold values from -60 to 60
- permittivity: float32 [3, 16, 1024], P(None, 'grid'), may hold values from 1 to 10
- labels: int32 [16, 1024], P('grid'), may hold values from 0 to 7
- sigma_table: float32 [8], replicated, may hold values from 0.1 to 10
Outputs:
- new_basis: float32 [128, 3, 16, 1024], P('cols', None, 'grid')
- coefficients: float32 [1024, 128], P('cols')
- cross_terms: float32 [3, 1024, 128], P(None, 'cols')
- block_terms: float32 [3, 128, 128], P(None, 'cols')
All inputs are finite; a program needn't handle non-finite values.
Results may differ from a plain program's by a relative error of at most 0.0003.
Values sent between devices are 32-bit elements; how exact they have to be, the bound alone decides.
A program may use at most 128 MiB of HBM per device.

v0:
```python
import jax
import jax.numpy as jnp
from jax import lax
from jax.sharding import PartitionSpec as P

NY = 32
HIGHEST = lax.Precision.HIGHEST


def padded(shard, sides, width):
    for axis, dim in sides:
        size, length = (lax.axis_size(axis), shard.shape[dim])
        up = [(i, (i + 1) % size) for i in range(size - 1)]
        down = [(j, i) for i, j in up]
        last = lax.slice_in_dim(shard, length - width, length, axis=dim)
        leading = lax.slice_in_dim(shard, 0, width, axis=dim)
        before = lax.ppermute(last, axis, up)
        after = lax.ppermute(leading, axis, down)
        shard = jnp.concatenate([before, shard, after], axis=dim)
    return shard


def cells_dot(left_rows, right_rows):
    left_flat = left_rows.reshape(left_rows.shape[0], -1)
    right_flat = right_rows.reshape(right_rows.shape[0], -1)
    return lax.dot_general(
        left_flat,
        right_flat,
        (((1,), (1,)), ((), ())),
        precision=HIGHEST,
        preferred_element_type=jnp.float32,
    )


def combine_rows(weights, fields):
    flattened = fields.reshape(fields.shape[0], -1)
    output_rows = lax.dot_general(
        weights,
        flattened,
        (((0,), (0,)), ((), ())),
        precision=HIGHEST,
        preferred_element_type=jnp.float32,
    )
    return output_rows.reshape((weights.shape[1],) + fields.shape[1:])


def forward_x(field, row_len):
    padding_cols = jnp.zeros(field.shape[:-1] + (row_len,), field.dtype)
    return jnp.concatenate([field[..., row_len:], padding_cols], axis=-1)


def backward_x(field, row_len):
    padding_cols = jnp.zeros(field.shape[:-1] + (row_len,), field.dtype)
    return jnp.concatenate([padding_cols, field[..., :-row_len]], axis=-1)


def forward_y(field, row_len):
    column_pos = lax.broadcasted_iota(jnp.int32, (field.shape[-1],), 0) % row_len
    padding_cols = jnp.zeros(field.shape[:-1] + (1,), field.dtype)
    shifted = jnp.concatenate([field[..., 1:], padding_cols], axis=-1)
    return jnp.where(column_pos != row_len - 1, shifted, 0.0)


def backward_y(field, row_len):
    column_pos = lax.broadcasted_iota(jnp.int32, (field.shape[-1],), 0) % row_len
    padding_cols = jnp.zeros(field.shape[:-1] + (1,), field.dtype)
    shifted = jnp.concatenate([padding_cols, field[..., :-1]], axis=-1)
    return jnp.where(column_pos != 0, shifted, 0.0)


def curl_curl(extended, row_len):
    field_x = extended[:, 0]
    field_y = extended[:, 1]
    field_z = extended[:, 2]

    def middle(field):
        return field[:, 1:-1]

    def plus_x(field):
        return forward_x(field, row_len) - field

    def minus_x(field):
        return field - backward_x(field, row_len)

    def plus_y(field):
        return forward_y(field, row_len) - field

    def minus_y(field):
        return field - backward_y(field, row_len)

    def second_x(field):
        return forward_x(field, row_len) - 2.0 * field + backward_x(field, row_len)

    def second_y(field):
        return forward_y(field, row_len) - 2.0 * field + backward_y(field, row_len)

    def second_z(field):
        return field[:, 2:] - 2.0 * field[:, 1:-1] + field[:, :-2]

    curl_x = (
        -second_y(middle(field_x))
        - second_z(field_x)
        + minus_y(plus_x(middle(field_y)))
        + plus_x(middle(field_z))
        - plus_x(field_z[:, :-2])
    )
    curl_y = (
        -second_x(middle(field_y))
        - second_z(field_y)
        + minus_x(plus_y(middle(field_x)))
        + plus_y(middle(field_z))
        - plus_y(field_z[:, :-2])
    )
    curl_z = (
        -second_x(middle(field_z))
        - second_y(middle(field_z))
        + minus_x(field_x[:, 2:] - middle(field_x))
        + minus_y(field_y[:, 2:] - middle(field_y))
    )
    return jnp.stack([curl_x, curl_y, curl_z], axis=1)


def lookup_sigma(labels, sigma_table):
    region_ids = jnp.arange(sigma_table.shape[0], dtype=jnp.int32)
    picked = jnp.where(labels[None] == region_ids[:, None, None], sigma_table[:, None, None], 0.0)
    return jnp.sum(picked, axis=0)


def apply_ops(fields, permittivity, conductivity):
    extended = padded(fields, (("grid", 2),), 1)
    curl_term = curl_curl(extended, NY)
    mass_term = permittivity[None] * fields
    loss_term = conductivity[None, None] * fields
    return (curl_term, mass_term, loss_term)


def shards(basis, snapshots, permittivity, labels, sigma_table):
    basis_cols = basis.shape[0]
    snap_cols = snapshots.shape[0]
    total_snap = snap_cols * lax.axis_size("cols")
    unknowns = 3 * snapshots.shape[3] * snapshots.shape[2] * lax.axis_size("grid")
    conductivity = lookup_sigma(labels, sigma_table)
    current = snapshots
    coefficients = jnp.zeros((basis_cols, total_snap), jnp.float32)
    for sweep_index in range(2):
        partial_value = cells_dot(basis, lax.all_gather(current, "cols", axis=0, tiled=True))
        coef_part = lax.psum(partial_value, "grid")
        current = current - lax.psum_scatter(
            combine_rows(coef_part, basis), "cols", scatter_dimension=0, tiled=True
        )
        coefficients = coefficients + coef_part
    finished = lax.all_gather(current, "cols", axis=0, tiled=True)
    own_start = lax.axis_index("cols") * snap_cols
    identity = jnp.eye(total_snap, dtype=jnp.float32)
    gram_sum = lax.psum(cells_dot(finished, finished) / unknowns, "grid")
    lower_factor = jnp.linalg.cholesky(gram_sum)
    inverse = jax.scipy.linalg.solve_triangular(lower_factor, identity, lower=True)
    new_all = combine_rows(inverse.T, finished)
    curl_term, mass_term, loss_term = apply_ops(new_all, permittivity, conductivity)
    own_new = lax.dynamic_slice_in_dim(new_all, own_start, snap_cols, 0)
    cross_part = jnp.stack(
        [cells_dot(basis, curl_term), cells_dot(basis, mass_term), cells_dot(basis, loss_term)],
        axis=0,
    )
    block_part = (
        jnp.stack(
            [
                cells_dot(own_new, curl_term),
                cells_dot(own_new, mass_term),
                cells_dot(own_new, loss_term),
            ],
            axis=0,
        )
        / unknowns
    )
    cross_terms, block_terms = lax.psum((cross_part, block_part), "grid")
    return (own_new, coefficients, cross_terms, block_terms)


def solution(mesh):
    placed = (
        P("cols", None, "grid", None),
        P("cols", None, "grid", None),
        P(None, "grid", None),
        P("grid", None),
        P(),
    )
    return jax.shard_map(
        shards,
        mesh=mesh,
        in_specs=placed,
        out_specs=(
            P("cols", None, "grid", None),
            P("cols", None),
            P(None, "cols", None),
            P(None, "cols", None),
        ),
        check_vma=False,
    )
```

profile of v0, /device:TPU:0, one launch (start us, length us, event | category | flops | bytes accessed | tf_op | source)
XLA Modules:
  0.0 642.6 jit_solution(8649278137576237144)
XLA Ops:
  7.2 2.3 copy.44
  9.5 0.0 all-reduce.19.cloned.1.call-start
  9.5 31.9 %all-gather.4.cloned.1.call-done = f32[128,3,2,1024]{3,0,2,1:T(8,128)} async-done(((f32[32,3,2,1024]{3,0,2,1:T(8,128)}), f32[128,3,2,1024]{3,0,2,1:T(8,128)}) %all-gather.4.cloned.1.call-update) | async-done | bytes 3145744 | tf_op jit(solution)/shard_map/all_gather | solution.py:146
  41.4 10.8 %fusion.23 = f32[256,128]{1,0:T(8,128)} fusion(f32[128,3,2,1024]{3,0,2,1:T(8,128)} %all-gather.4.cloned.1.call-done, f32[256,3,2,1024]{3,2,1,0:T(2,128)} %param.5), kind=kOutput, calls=%fused_computation.28 | convolution fusion | flops 2415919104 | bytes 9568256 | tf_op jit(solution)/shard_map/dot_general | solution.py:26
  52.2 0.0 reduce-scatter.3.cloned.1.call-start
  52.2 9.0 %reshape.49 = f32[256,6144]{1,0:T(8,128)} reshape(f32[256,3,2,1024]{3,2,1,0:T(2,128)} %param.5) | data formatting | bytes 12582912 | tf_op jit(solution)/shard_map/reshape | solution.py:24
  61.2 6.6 %copy.42 = f32[6144,256]{1,0:T(8,128)} copy(f32[6144,256]{0,1:T(8,128)} %bitcast.112) | data formatting | bytes 12582912 | tf_op jit(solution)/shard_map/dot_general | solution.py:37
  67.8 54.2 %all-reduce.19.cloned.1.call-done = f32[256,128]{1,0:T(8,128)} async-done(((f32[256,128]{1,0:T(8,128)}), f32[256,128]{1,0:T(8,128)}) %all-reduce.19.cloned.1.call-update) | async-done | bytes 131088 | tf_op jit(solution)/shard_map/psum | solution.py:147
  122.0 11.2 %fusion.63 = f32[128,3,2,1024]{3,0,2,1:T(8,128)} fusion(f32[3,2,1024,256]{3,2,1,0:T(8,128)} %bitcast.110, f32[256,128]{1,0:T(8,128)} %all-reduce.19.cloned.1.call-done), kind=kOutput, calls=%fused_computation.61 | convolution fusion | flops 2415919104 | bytes 9568256 | tf_op jit(solution)/shard_map/dot_general | solution.py:37
  133.3 0.3 all-gather.6.cloned.1.call-start
  133.6 37.1 %reduce-scatter.3.cloned.1.call-done = f32[32,3,2,1024]{3,0,2,1:T(8,128)} async-done(((f32[128,3,2,1024]{3,0,2,1:T(8,128)}), f32[32,3,2,1024]{3,0,2,1:T(8,128)}) %reduce-scatter.3.cloned.1.call-update) | async-done | bytes 786448 | tf_op jit(solution)/shard_map/reduce_scatter | solution.py:148
  170.7 2.3 copy_subtract_fusion
  173.0 0.0 all-reduce.21.cloned.1.call-start
  173.1 28.6 %all-gather.6.cloned.1.call-done = f32[128,3,2,1024]{3,0,2,1:T(8,128)} async-done(((f32[32,3,2,1024]{3,0,2,1:T(8,128)}), f32[128,3,2,1024]{3,0,2,1:T(8,128)}) %all-gather.6.cloned.1.call-update) | async-done | bytes 3145744 | tf_op jit(solution)/shard_map/all_gather | solution.py:146
  201.7 10.7 %fusion.26 = f32[256,128]{1,0:T(8,128)} fusion(f32[128,3,2,1024]{3,0,2,1:T(8,128)} %all-gather.6.cloned.1.call-done, f32[256,3,2,1024]{3,2,1,0:T(2,128)} %param.5), kind=kOutput, calls=%fused_computation.29 | convolution fusion | flops 2415919104 | bytes 9568256 | tf_op jit(solution)/shard_map/dot_general | solution.py:26
  212.4 0.0 reduce-scatter.5.cloned.1.call-start
  212.4 69.8 %all-reduce.21.cloned.1.call-done = f32[256,128]{1,0:T(8,128)} async-done(((f32[256,128]{1,0:T(8,128)}), f32[256,128]{1,0:T(8,128)}) %all-reduce.21.cloned.1.call-update) | async-done | bytes 131088 | tf_op jit(solution)/shard_map/psum | solution.py:147
  282.2 11.2 %fusion.61 = f32[128,3,2,1024]{3,0,2,1:T(8,128)} fusion(f32[3,2,1024,256]{3,2,1,0:T(8,128)} %bitcast.111, f32[256,128]{1,0:T(8,128)} %all-reduce.21.cloned.1.call-done), kind=kOutput, calls=%fused_computation.59 | convolution fusion | flops 2415919104 | bytes 9568256 | tf_op jit(solution)/shard_map/dot_general | solution.py:37
  293.5 0.0 all-gather.8.cloned.1.call-start
  293.5 37.3 %reduce-scatter.5.cloned.1.call-done = f32[32,3,2,1024]{3,0,2,1:T(8,128)} async-done(((f32[128,3,2,1024]{3,0,2,1:T(8,128)}), f32[32,3,2,1024]{3,0,2,1:T(8,128)}) %reduce-scatter.5.cloned.1.call-update) | async-done | bytes 786448 | tf_op jit(solution)/shard_map/reduce_scatter | solution.py:148
  330.9 2.1 sub.76
  333.0 0.4 all-reduce.23.cloned.1.call-start
  333.4 28.2 %all-gather.8.cloned.1.call-done = f32[128,3,2,1024]{3,0,2,1:T(8,128)} async-done(((f32[32,3,2,1024]{3,0,2,1:T(8,128)}), f32[128,3,2,1024]{3,0,2,1:T(8,128)}) %all-gather.8.cloned.1.call-update) | async-done | bytes 3145744 | tf_op jit(solution)/shard_map/all_gather | solution.py:152
  361.7 6.3 fusion.42
  368.0 0.0 all-reduce.25.cloned.1.call-start
  368.0 2.3 copy.50
  370.4 66.2 %all-reduce.23.cloned.1.call-done = f32[128,128]{0,1:T(8,128)} async-done(((f32[128,128]{0,1:T(8,128)}), f32[128,128]{0,1:T(8,128)}) %all-reduce.23.cloned.1.call-update) | async-done | bytes 65552 | tf_op jit(solution)/shard_map/psum | solution.py:155
  436.6 0.9 copy.49
  437.5 0.9 fusion.67
  438.4 11.7 %cholesky.17 = f32[128,128]{1,0:T(8,128)S(1)} custom-call(f32[128,128]{1,0:T(8,128)S(1)} %fusion.67), custom_call_target="Cholesky" | custom-call | tf_op jit(solution)/shard_map/jit(cholesky)/cholesky | solution.py:156
  450.1 0.6 compare_reduce_fusion
  450.8 0.7 fusion.65
  451.4 9.8 %custom-call.7 = f32[1,128,128]{1,2,0:T(8,128)S(1)} custom-call(f32[1,128,128]{2,1,0:T(8,128)S(1)} %fusion.65), custom_call_target="InvertDiagBlocksLowerTriangular" | custom-call | tf_op jit(solution)/shard_map/jit(_solve_triangular)/triangular_solve | solution.py:157
  461.3 0.2 convolution_bitcast_fusion
  461.5 4.7 fusion.10
  466.2 1.9 fusion.75
  468.1 4.5 collective-permute-start
  472.6 1.5 collective-permute-start.1
  474.1 0.1 select_reduce_fusion
  474.2 0.7 add.132
  474.9 0.1 constant_dynamic-slice_fusion
  475.0 0.9 copy-done.1
  475.8 3.1 fusion.44
  479.0 9.9 %fusion.37 = f32[1,256,128]{1,2,0:T(8,128)S(1)} fusion(f32[256,3,2,1024]{3,2,1,0:T(2,128)} %param.5, f32[128,3,2,1024]{3,0,2,1:T(8,128)S(1)} %fusion.10, f32[2,1024]{1,0:T(2,128)S(1)} %select_reduce_fusion), kind=kOutput, calls=%fused_computation.32 | convolution fusion | flops 2416705536 | bytes 9576448 | tf_op jit(solution)/shard_map/dot_general | solution.py:26
  488.9 7.2 %fusion.32 = f32[1,256,128]{1,2,0:T(8,128)S(1)} fusion(f32[256,3,2,1024]{3,2,1,0:T(2,128)S(1)} %bitcast.109, f32[128,3,2,1024]{3,0,2,1:T(8,128)S(1)} %fusion.10, f32[3,2,1024]{2,1,0:T(2,128)S(1)} %copy-done.15), kind=kOutput, calls=%fused_computation.31 | convolution fusion | flops 2416705536 | bytes 9592832 | tf_op jit(solution)/shard_map/dot_general | solution.py:26
  496.2 41.0 %collective-permute-done = f32[128,3,1,1024]{3,0,2,1:T(8,128)} collective-permute-done((f32[128,3,1,1024]{3,0,2,1:T(8,128)}, f32[128,3,1,1024]{3,0,2,1:T(8,128)}, u32[]{:S(2)}, u32[]{:S(2)}) %collective-permute-start) | collective-permute-done | bytes 1572896 | tf_op jit(solution)/shard_map/ppermute | solution.py:17
  537.2 2.7 pad_maximum_fusion
  539.9 1.1 slice_bitcast_fusion
  541.1 2.6 fusion.76
  543.7 2.4 fusion.77
  546.1 0.4 pad_subtract_fusion
  546.5 3.4 fusion.59
  549.9 1.4 fusion.54
  551.3 0.2 copy-done.8
  551.4 0.3 copy-done.11
  551.8 1.2 add_bitcast_fusion
  553.0 7.3 %fusion.29 = f32[1,256,128]{1,2,0:T(8,128)S(1)} fusion(f32[256,3,2,1024]{3,2,1,0:T(2,128)S(1)} %bitcast.109, f32[128,1,2,1024]{3,0,2,1:T(8,128)S(1)} %add_bitcast_fusion, f32[128,1,2,1024]{3,0,2,1:T(8,128)S(1)} %fusion.54, f32[128,1,2,1024]{3,0,2,1:T(8,128)S(1)} %get-tuple-element.19), kind=kOutput, calls=%fused_computation.30 | convolution fusion | flops 2417491968 | bytes 9568256 | tf_op jit(solution)/shard_map/dot_general | solution.py:26
  560.3 0.8 pad_maximum_fusion.8
  561.2 4.4 fusion.47
  565.6 1.5 copy.54
  567.1 3.1 fusion.43
  570.3 37.2 %psum.39 = f32[3,32,128]{2,1,0:T(8,128)} all-reduce(f32[3,32,128]{2,1,0:T(8,128)S(1)} %maximum_multiply_fusion), channel_id=1, replica_groups=mesh['grid'=8,'cols'=4] {'grid'}, use_global_device_ids=true, to_apply=%region_9.10 | all-reduce | flops 12288 | bytes 98304 | tf_op jit(solution)/shard_map/psum | solution.py:176
  607.5 26.2 %all-reduce.25.cloned.1.call-done = f32[3,256,128]{1,2,0:T(8,128)} async-done(((f32[3,256,128]{1,2,0:T(8,128)}), f32[3,256,128]{1,2,0:T(8,128)}) %all-reduce.25.cloned.1.call-update) | async-done | bytes 393232 | tf_op jit(solution)/shard_map/psum | solution.py:176
  633.7 1.9 copy.55
  (52 shorter events, 0.3 us)
Async XLA Ops:
  7.2 34.2 %all-gather.4.cloned.1.call-start = ((), (), s32[]{:S(2)}) async-start(), calls=%async_computation.2 | async-start | bytes 3932160 | tf_op jit(solution)/shard_map/all_gather | solution.py:146
  9.5 112.6 %all-reduce.19.cloned.1.call-start = ((), (), s32[]{:S(2)}) async-start(), calls=%async_computation.3 | async-start | bytes 262144 | tf_op jit(solution)/shard_map/psum | solution.py:147
  52.2 118.5 %reduce-scatter.3.cloned.1.call-start = ((), (), s32[]{:S(2)}) async-start(), calls=%async_computation.4 | async-start | bytes 3932160 | tf_op jit(solution)/shard_map/reduce_scatter | solution.py:148
  133.3 37.4 %copy-start.12 = (f32[32,3,2,1024]{3,2,1,0:T(2,128)S(1)}, f32[32,3,2,1024]{3,2,1,0:T(2,128)}, u32[]{:S(2)}) copy-start(f32[32,3,2,1024]{3,2,1,0:T(2,128)} %param.6) | copy-start | bytes 2359300
  133.3 68.4 %all-gather.6.cloned.1.call-start = ((), (), s32[]{:S(2)}) async-start(), calls=%async_computation.5 | async-start | bytes 3932160 | tf_op jit(solution)/shard_map/all_gather | solution.py:146
  173.0 109.2 %all-reduce.21.cloned.1.call-start = ((), (), s32[]{:S(2)}) async-start(), calls=%async_computation.6 | async-start | bytes 262144 | tf_op jit(solution)/shard_map/psum | solution.py:147
  212.4 118.5 %reduce-scatter.5.cloned.1.call-start = ((), (), s32[]{:S(2)}) async-start(), calls=%async_computation.7 | async-start | bytes 3932160 | tf_op jit(solution)/shard_map/reduce_scatter | solution.py:148
  293.5 37.4 %copy-start.3 = (f32[32,3,2,1024]{3,0,2,1:T(8,128)S(1)}, f32[32,3,2,1024]{3,0,2,1:T(8,128)}, u32[]{:S(2)}) copy-start(f32[32,3,2,1024]{3,0,2,1:T(8,128)} %copy_subtract_fusion) | copy-start | bytes 2359300
  293.5 68.2 %all-gather.8.cloned.1.call-start = ((), (), s32[]{:S(2)}) async-start(), calls=%async_computation.8 | async-start | bytes 3932160 | tf_op jit(solution)/shard_map/all_gather | solution.py:152
  333.0 103.6 %all-reduce.23.cloned.1.call-start = ((), (), s32[]{:S(2)}) async-start(), calls=%async_computation.9 | async-start | bytes 131072 | tf_op jit(solution)/shard_map/psum | solution.py:155
  361.7 6.4 copy-start
  368.0 265.7 %all-reduce.25.cloned.1.call-start = ((), (), s32[]{:S(2)}) async-start(), calls=%async_computation.10 | async-start | bytes 786432 | tf_op jit(solution)/shard_map/psum | solution.py:176
  466.2 7.9 %copy-start.16 = (s32[2,1024]{1,0:T(2,128)S(1)}, s32[2,1024]{1,0:T(2,128)}, u32[]{:S(2)}) copy-start(s32[2,1024]{1,0:T(2,128)} %param.8) | copy-start | bytes 24580
  466.2 7.9 %copy-start.17 = (f32[8]{0:T(128)S(1)}, f32[8]{0:T(128)}, u32[]{:S(2)}) copy-start(f32[8]{0:T(128)} %param.9) | copy-start | bytes 100
  466.2 8.0 %copy-start.13 = (f32[256,128]{1,0:T(8,128)S(1)}, f32[256,128]{1,0:T(8,128)}, u32[]{:S(2)}) copy-start(f32[256,128]{1,0:T(8,128)} %all-reduce.19.cloned.1.call-done) | copy-start | bytes 393220
  466.2 8.0 %copy-start.14 = (f32[256,128]{1,0:T(8,128)S(1)}, f32[256,128]{1,0:T(8,128)}, u32[]{:S(2)}) copy-start(f32[256,128]{1,0:T(8,128)} %all-reduce.21.cloned.1.call-done) | copy-start | bytes 393220
  466.2 9.6 %copy-start.15 = (f32[3,2,1024]{2,1,0:T(2,128)S(1)}, f32[3,2,1024]{2,1,0:T(2,128)}, u32[]{:S(2)}) copy-start(f32[3,2,1024]{2,1,0:T(2,128)} %param.7) | copy-start | bytes 73732
  468.1 69.1 %collective-permute-start = (f32[128,3,1,1024]{3,0,2,1:T(8,128)}, f32[128,3,1,1024]{3,0,2,1:T(8,128)}, u32[]{:S(2)}, u32[]{:S(2)}) collective-permute-start(f32[128,3,1,1024]{3,0,2,1:T(8,128)} %get-tuple-element.21), channel_id=1, source_target_pairs={{0,4},{4,8},{8,12},{12,16},{16,20},{20,24},{24,28},{1,5},{5,9},{9,... | collective-permute-start | bytes 4718600 | tf_op jit(solution)/shard_map/ppermute | solution.py:17
  472.6 64.6 %collective-permute-start.1 = (f32[128,3,1,1024]{3,0,2,1:T(8,128)}, f32[128,3,1,1024]{3,0,2,1:T(8,128)}, u32[]{:S(2)}, u32[]{:S(2)}) collective-permute-start(f32[128,3,1,1024]{3,0,2,1:T(8,128)} %get-tuple-element.22), channel_id=1, source_target_pairs={{4,0},{8,4},{12,8},{16,12},{20,16},{24,20},{28,24},{5,1},{9,5},{13... | collective-permute-start | bytes 4718600 | tf_op jit(solution)/shard_map/ppermute | solution.py:18
  475.0 0.9 copy-start.1
  475.8 13.0 %slice-start = ((s8[6291456]{0:T(1024)(128)(4,1)}), s8[4194304]{0:T(1024)(128)(4,1)S(1)}, s32[]{:S(2)}) async-start(s8[6291456]{0:T(1024)(128)(4,1)} %bitcast.108), calls=%async_computation.11 | async-start | bytes 8388608
  479.0 9.9 %slice-start.1 = ((s8[6291456]{0:T(1024)(128)(4,1)}), s8[2097152]{0:T(1024)(128)(4,1)S(1)}, s32[]{:S(2)}) async-start(s8[6291456]{0:T(1024)(128)(4,1)} %bitcast.108), calls=%async_computation.12 | async-start | bytes 4194304
  549.8 3.2 copy-start.6
  549.8 1.6 copy-start.8
  549.8 1.9 copy-start.11
  551.2 1.8 copy-start.4
  553.0 7.3 %copy-start.9 = (f32[128,1,2,1024]{3,0,2,1:T(8,128)}, f32[128,1,2,1024]{3,0,2,1:T(8,128)S(1)}, u32[]{:S(2)}) copy-start(f32[128,1,2,1024]{3,0,2,1:T(8,128)S(1)} %add_bitcast_fusion) | copy-start | bytes 3145732
  561.1 4.5 copy-start.2
  561.1 6.0 copy-start.5
  561.1 6.0 copy-start.7
  561.1 6.0 copy-start.10
Sparse Core Ops, SparseCore 0:
  10.1 31.2 all-gather.3
  52.3 69.6 all-reduce.18
  133.4 37.2 reduce-scatter.2
  173.1 28.5 all-gather.5
  212.5 69.6 all-reduce.20
  293.6 37.2 reduce-scatter.4
  333.1 28.5 all-gather.7
  368.1 68.4 all-reduce.22
  561.2 72.4 all-reduce.24
where the time goes:
time: 652 us; the launch traced here: 643 us
  waiting for transfers between devices  421 us (65%)
  matrix products  90.2 us (14%)
  other arithmetic  38.7 us (6%)
  blocking collectives  37.2 us (6%)
  local copies, waits for them, and re-layouts  34 us (5%)
  between operations  14.7 us (2%)
  starting transfers between devices  6.98 us (1%)
    psum x2, waiting for transfers between devices, shards(): coef_part = lax.psum(partial_value, 'grid')  124 us
    reduce_scatter x2, waiting for transfers between devices, shards(): lax.psum_scatter(combine_rows(coef_part, basis), 'cols', scatter_dimensio...  74.4 us
    psum x1, waiting for transfers between devices, shards(): gram_sum = lax.psum(cells_dot(finished, finished) / unknowns, 'grid')  66.2 us
    dot_general x9, matrix products, cells_dot(): lax.dot_general(left_flat, right_flat, (((1,), (1,)), ((), ())), precisio...  62.8 us
    all_gather x2, waiting for transfers between devices, shards(): lax.all_gather(current, 'cols', axis=0, tiled=True)  60.5 us
    ppermute x1, waiting for transfers between devices, padded(): before = lax.ppermute(last, axis, up)  41 us
    psum x1, blocking collectives, shards(): cross_terms, block_terms = lax.psum((cross_part, block_part), 'grid')  37.2 us
    all_gather x1, waiting for transfers between devices, shards(): finished = lax.all_gather(current, 'cols', axis=0, tiled=True)  28.2 us
  transfers between devices with their start and end apart: 11, of which 10 were waited for; matrix products, arithmetic and copies ran while one was open for 7% of the time, Pallas kernels for 0%

commit v1 on v0

--- a/solution.py
+++ b/solution.py
@@ -5,6 +5,11 @@
 
 NY = 32
 HIGHEST = lax.Precision.HIGHEST
+
+
+def recover_slot(shard_in):
+    lower = jnp.sum(jax.lax.all_gather(shard_in, axis_name="grid"), 0)
+    return lower
 
 
 def padded(shard, sides, width):
@@ -144,7 +149,7 @@
     coefficients = jnp.zeros((basis_cols, total_snap), jnp.float32)
     for sweep_index in range(2):
         partial_value = cells_dot(basis, lax.all_gather(current, "cols", axis=0, tiled=True))
-        coef_part = lax.psum(partial_value, "grid")
+        coef_part = recover_slot(partial_value)
         current = current - lax.psum_scatter(
             combine_rows(coef_part, basis), "cols", scatter_dimension=0, tiled=True
         )

time: 652 us -> 594 us (0.911)
  waiting for transfers between devices: 421 us -> 359 us
    psum x2 -> x0, waiting for transfers between devices: 124 us -> none  [shards(): coef_part = lax.psum(partial_value, 'grid')]
    all_gather x0 -> x2, waiting for transfers between devices: none -> 64.2 us  [recover_slot(): lower = jnp.sum(jax.lax.all_gather(shard_in, axis_name='grid'), 0)]
  transfers between devices with their start and end apart: 11 -> 11, of which waited for: 10 -> 10; matrix products, arithmetic and copies ran while one was open for 7% -> 8% of each run, Pallas kernels for 0% -> 0%
where the time goes in v1:
time: 594 us; the launch traced here: 585 us
  waiting for transfers between devices  359 us (60%)
  matrix products  91.3 us (15%)
  other arithmetic  40.3 us (7%)
  blocking collectives  37.2 us (6%)
  local copies, waits for them, and re-layouts  35.7 us (6%)
  between operations  14.5 us (2%)
  starting transfers between devices  7.45 us (1%)
    reduce_scatter x2, waiting for transfers between devices, shards(): lax.psum_scatter(combine_rows(coef_part, basis), 'cols', scatter_dimensio...  73.3 us
    psum x1, waiting for transfers between devices, shards(): gram_sum = lax.psum(cells_dot(finished, finished) / unknowns, 'grid')  66 us
    dot_general x9, matrix products, cells_dot(): lax.dot_general(left_flat, right_flat, (((1,), (1,)), ((), ())), precisio...  64.3 us
    all_gather x2, waiting for transfers between devices, recover_slot(): lower = jnp.sum(jax.lax.all_gather(shard_in, axis_name='grid'), 0)  64.2 us
    all_gather x2, waiting for transfers between devices, shards(): lax.all_gather(current, 'cols', axis=0, tiled=True)  60.5 us
    ppermute x1, waiting for transfers between devices, padded(): before = lax.ppermute(last, axis, up)  39.9 us
    psum x1, blocking collectives, shards(): cross_terms, block_terms = lax.psum((cross_part, block_part), 'grid')  37.2 us
    all_gather x1, waiting for transfers between devices, shards(): finished = lax.all_gather(current, 'cols', axis=0, tiled=True)  28.6 us
  transfers between devices with their start and end apart: 11, of which 10 were waited for; matrix products, arithmetic and copies ran while one was open for 8% of the time, Pallas kernels for 0%

profile of v1, /device:TPU:0, one launch (start us, length us, event | category | flops | bytes accessed | tf_op | source)
XLA Modules:
  0.0 585.3 jit_solution(11706559846571948665)
XLA Ops:
  7.2 2.3 copy.71
  9.5 31.9 %all-gather.8.cloned.1.call-done = f32[128,3,2,1024]{3,0,2,1:T(8,128)} async-done(((f32[32,3,2,1024]{3,0,2,1:T(8,128)}), f32[128,3,2,1024]{3,0,2,1:T(8,128)}) %all-gather.8.cloned.1.call-update) | async-done | bytes 3145744 | tf_op jit(solution)/shard_map/all_gather | solution.py:151
  41.4 10.8 %fusion.23 = f32[256,128]{1,0:T(8,128)} fusion(f32[128,3,2,1024]{3,0,2,1:T(8,128)} %all-gather.8.cloned.1.call-done, f32[256,3,2,1024]{3,2,1,0:T(2,128)} %param.5), kind=kOutput, calls=%fused_computation.28 | convolution fusion | flops 2415919104 | bytes 9568256 | tf_op jit(solution)/shard_map/dot_general | solution.py:31
  52.2 9.0 %reshape.49 = f32[256,6144]{1,0:T(8,128)} reshape(f32[256,3,2,1024]{3,2,1,0:T(2,128)} %param.5) | data formatting | bytes 12582912 | tf_op jit(solution)/shard_map/reshape | solution.py:29
  61.2 6.6 %copy.69 = f32[6144,256]{1,0:T(8,128)} copy(f32[6144,256]{0,1:T(8,128)} %bitcast.122) | data formatting | bytes 12582912 | tf_op jit(solution)/shard_map/dot_general | solution.py:42
  67.8 24.8 %all-gather.14.cloned.1.call-done = f32[2048,128]{1,0:T(8,128)} async-done(((f32[256,128]{1,0:T(8,128)}), f32[2048,128]{1,0:T(8,128)}) %all-gather.14.cloned.1.call-update) | async-done | bytes 1048592 | tf_op jit(solution)/shard_map/all_gather | solution.py:11
  92.6 1.3 reduce_sum.27
  93.9 11.2 %fusion.63 = f32[128,3,2,1024]{3,0,2,1:T(8,128)} fusion(f32[3,2,1024,256]{3,2,1,0:T(8,128)} %bitcast.120, f32[256,128]{1,0:T(8,128)S(1)} %reduce_sum.27), kind=kOutput, calls=%fused_computation.62 | convolution fusion | flops 2415919104 | bytes 9568256 | tf_op jit(solution)/shard_map/dot_general | solution.py:42
  105.0 0.5 all-gather.10.cloned.1.call-start
  105.6 36.4 %reduce-scatter.3.cloned.1.call-done = f32[32,3,2,1024]{3,0,2,1:T(8,128)} async-done(((f32[128,3,2,1024]{3,0,2,1:T(8,128)}), f32[32,3,2,1024]{3,0,2,1:T(8,128)}) %reduce-scatter.3.cloned.1.call-update) | async-done | bytes 786448 | tf_op jit(solution)/shard_map/reduce_scatter | solution.py:153
  141.9 2.3 copy_subtract_fusion
  144.3 28.6 %all-gather.10.cloned.1.call-done = f32[128,3,2,1024]{3,0,2,1:T(8,128)} async-done(((f32[32,3,2,1024]{3,0,2,1:T(8,128)}), f32[128,3,2,1024]{3,0,2,1:T(8,128)}) %all-gather.10.cloned.1.call-update) | async-done | bytes 3145744 | tf_op jit(solution)/shard_map/all_gather | solution.py:151
  172.9 11.4 %fusion.26 = f32[256,128]{0,1:T(8,128)} fusion(f32[128,3,2,1024]{3,0,2,1:T(8,128)} %all-gather.10.cloned.1.call-done, f32[256,3,2,1024]{3,2,1,0:T(2,128)} %param.5), kind=kOutput, calls=%fused_computation.29 | convolution fusion | flops 2415919104 | bytes 9568256 | tf_op jit(solution)/shard_map/dot_general | solution.py:31
  184.3 0.2 reduce-scatter.5.cloned.1.call-start
  184.6 39.5 %all-gather.16.cloned.1.call-done = f32[2048,128]{0,1:T(8,128)} async-done(((f32[256,128]{0,1:T(8,128)}), f32[2048,128]{0,1:T(8,128)}) %all-gather.16.cloned.1.call-update) | async-done | bytes 1048592 | tf_op jit(solution)/shard_map/all_gather | solution.py:11
  224.0 1.6 copy.96
  225.6 0.3 bitcast_reduce_fusion
  225.9 10.9 %fusion.61 = f32[128,3,2,1024]{3,0,2,1:T(8,128)} fusion(f32[3,2,1024,256]{3,2,1,0:T(8,128)} %bitcast.121, f32[256,128]{0,1:T(8,128)S(1)} %bitcast_reduce_fusion), kind=kOutput, calls=%fused_computation.60 | convolution fusion | flops 2415919104 | bytes 9568256 | tf_op jit(solution)/shard_map/dot_general | solution.py:42
  236.8 0.0 all-gather.12.cloned.1.call-start
  236.9 36.9 %reduce-scatter.5.cloned.1.call-done = f32[32,3,2,1024]{3,0,2,1:T(8,128)} async-done(((f32[128,3,2,1024]{3,0,2,1:T(8,128)}), f32[32,3,2,1024]{3,0,2,1:T(8,128)}) %reduce-scatter.5.cloned.1.call-update) | async-done | bytes 786448 | tf_op jit(solution)/shard_map/reduce_scatter | solution.py:153
  273.8 2.1 sub.76
  276.0 28.6 %all-gather.12.cloned.1.call-done = f32[128,3,2,1024]{3,0,2,1:T(8,128)} async-done(((f32[32,3,2,1024]{3,0,2,1:T(8,128)}), f32[128,3,2,1024]{3,0,2,1:T(8,128)}) %all-gather.12.cloned.1.call-update) | async-done | bytes 3145744 | tf_op jit(solution)/shard_map/all_gather | solution.py:157
  304.6 6.3 %fusion.42 = f32[128,128]{0,1:T(8,128)} fusion(f32[128,3,2,1024]{3,0,2,1:T(8,128)} %all-gather.12.cloned.1.call-done), kind=kOutput, calls=%fused_computation.35 | convolution fusion | flops 1207975936 | bytes 3211264 | tf_op jit(solution)/shard_map/dot_general | solution.py:31
  310.9 0.3 all-reduce.19.cloned.1.call-start
  311.2 2.3 copy.75
  313.5 66.0 %all-reduce.17.cloned.1.call-done = f32[128,128]{0,1:T(8,128)} async-done(((f32[128,128]{0,1:T(8,128)}), f32[128,128]{0,1:T(8,128)}) %all-reduce.17.cloned.1.call-update) | async-done | bytes 65552 | tf_op jit(solution)/shard_map/psum | solution.py:160
  379.6 0.9 copy.74
  380.5 0.9 fusion.67
  381.4 11.7 %cholesky.17 = f32[128,128]{1,0:T(8,128)S(1)} custom-call(f32[128,128]{1,0:T(8,128)S(1)} %fusion.67), custom_call_target="Cholesky" | custom-call | tf_op jit(solution)/shard_map/jit(cholesky)/cholesky | solution.py:161
  393.1 0.6 compare_reduce_fusion
  393.8 0.7 fusion.65
  394.4 9.8 %custom-call.7 = f32[1,128,128]{1,2,0:T(8,128)S(1)} custom-call(f32[1,128,128]{2,1,0:T(8,128)S(1)} %fusion.65), custom_call_target="InvertDiagBlocksLowerTriangular" | custom-call | tf_op jit(solution)/shard_map/jit(_solve_triangular)/triangular_solve | solution.py:162
  404.2 0.2 convolution_bitcast_fusion
  404.5 4.7 fusion.10
  409.2 1.8 fusion.75
  411.0 4.5 collective-permute-start
  415.6 1.7 collective-permute-start.1
  417.3 0.1 select_reduce_fusion
  417.4 0.1 copy.76
  417.5 0.7 add.128
  418.2 0.1 constant_dynamic-slice_fusion
  418.2 0.9 copy-done.1
  419.1 4.0 fusion.44
  423.2 9.9 %fusion.37 = f32[1,256,128]{1,2,0:T(8,128)S(1)} fusion(f32[256,3,2,1024]{3,2,1,0:T(2,128)} %param.5, f32[128,3,2,1024]{3,0,2,1:T(8,128)S(1)} %fusion.10, f32[2,1024]{1,0:T(2,128)S(1)} %select_reduce_fusion), kind=kOutput, calls=%fused_computation.32 | convolution fusion | flops 2416705536 | bytes 9576448 | tf_op jit(solution)/shard_map/dot_general | solution.py:31
  433.1 7.2 %fusion.32 = f32[1,256,128]{1,2,0:T(8,128)S(1)} fusion(f32[256,3,2,1024]{3,2,1,0:T(2,128)S(1)} %bitcast.119, f32[128,3,2,1024]{3,0,2,1:T(8,128)S(1)} %fusion.10, f32[3,2,1024]{2,1,0:T(2,128)S(1)} %copy-done.13), kind=kOutput, calls=%fused_computation.31 | convolution fusion | flops 2416705536 | bytes 9592832 | tf_op jit(solution)/shard_map/dot_general | solution.py:31
  440.3 39.9 %collective-permute-done = f32[128,3,1,1024]{3,0,2,1:T(8,128)} collective-permute-done((f32[128,3,1,1024]{3,0,2,1:T(8,128)}, f32[128,3,1,1024]{3,0,2,1:T(8,128)}, u32[]{:S(2)}, u32[]{:S(2)}) %collective-permute-start) | collective-permute-done | bytes 1572896 | tf_op jit(solution)/shard_map/ppermute | solution.py:22
  480.1 2.7 pad_maximum_fusion
  482.9 1.1 slice_bitcast_fusion
  484.0 2.6 fusion.76
  486.6 2.5 fusion.77
  489.1 0.4 pad_subtract_fusion
  489.4 3.4 fusion.59
  492.8 1.4 fusion.54
  494.2 0.2 copy-done.8
  494.4 0.3 copy-done.11
  494.7 1.2 add_bitcast_fusion
  496.0 7.2 %fusion.29 = f32[1,256,128]{1,2,0:T(8,128)S(1)} fusion(f32[256,3,2,1024]{3,2,1,0:T(2,128)S(1)} %bitcast.119, f32[128,1,2,1024]{3,0,2,1:T(8,128)S(1)} %add_bitcast_fusion, f32[128,1,2,1024]{3,0,2,1:T(8,128)S(1)} %fusion.54, f32[128,1,2,1024]{3,0,2,1:T(8,128)S(1)} %get-tuple-element.27), kind=kOutput, calls=%fused_computation.30 | convolution fusion | flops 2417491968 | bytes 9568256 | tf_op jit(solution)/shard_map/dot_general | solution.py:31
  503.2 0.8 pad_maximum_fusion.8
  504.1 4.4 fusion.47
  508.5 1.5 copy.80
  510.0 3.1 fusion.43
  513.2 37.2 %psum.23 = f32[3,32,128]{2,1,0:T(8,128)} all-reduce(f32[3,32,128]{2,1,0:T(8,128)S(1)} %maximum_multiply_fusion), channel_id=1, replica_groups=mesh['grid'=8,'cols'=4] {'grid'}, use_global_device_ids=true, to_apply=%region_9.10 | all-reduce | flops 12288 | bytes 98304 | tf_op jit(solution)/shard_map/psum | solution.py:181
  550.4 26.2 %all-reduce.19.cloned.1.call-done = f32[3,256,128]{1,2,0:T(8,128)} async-done(((f32[3,256,128]{1,2,0:T(8,128)}), f32[3,256,128]{1,2,0:T(8,128)}) %all-reduce.19.cloned.1.call-update) | async-done | bytes 393232 | tf_op jit(solution)/shard_map/psum | solution.py:181
  576.6 1.9 copy.81
  (52 shorter events, 0.5 us)
Async XLA Ops:
  7.2 34.2 %all-gather.8.cloned.1.call-start = ((), (), s32[]{:S(2)}) async-start(), calls=%async_computation.2 | async-start | bytes 3932160 | tf_op jit(solution)/shard_map/all_gather | solution.py:151
  9.5 83.1 %all-gather.14.cloned.1.call-start = ((), (), s32[]{:S(2)}) async-start(), calls=%async_computation.9 | async-start | bytes 1179648 | tf_op jit(solution)/shard_map/all_gather | solution.py:11
  52.2 89.7 %reduce-scatter.3.cloned.1.call-start = ((), (), s32[]{:S(2)}) async-start(), calls=%async_computation.3 | async-start | bytes 3932160 | tf_op jit(solution)/shard_map/reduce_scatter | solution.py:153
  105.0 36.9 %copy-start.12 = (f32[32,3,2,1024]{3,2,1,0:T(2,128)S(1)}, f32[32,3,2,1024]{3,2,1,0:T(2,128)}, u32[]{:S(2)}) copy-start(f32[32,3,2,1024]{3,2,1,0:T(2,128)} %param.6) | copy-start | bytes 2359300
  105.0 67.9 %all-gather.10.cloned.1.call-start = ((), (), s32[]{:S(2)}) async-start(), calls=%async_computation.4 | async-start | bytes 3932160 | tf_op jit(solution)/shard_map/all_gather | solution.py:151
  144.3 79.8 %all-gather.16.cloned.1.call-start = ((), (), s32[]{:S(2)}) async-start(), calls=%async_computation.10 | async-start | bytes 1179648 | tf_op jit(solution)/shard_map/all_gather | solution.py:11
  184.3 89.5 %reduce-scatter.5.cloned.1.call-start = ((), (), s32[]{:S(2)}) async-start(), calls=%async_computation.5 | async-start | bytes 3932160 | tf_op jit(solution)/shard_map/reduce_scatter | solution.py:153
  236.8 37.0 %copy-start.3 = (f32[32,3,2,1024]{3,0,2,1:T(8,128)S(1)}, f32[32,3,2,1024]{3,0,2,1:T(8,128)}, u32[]{:S(2)}) copy-start(f32[32,3,2,1024]{3,0,2,1:T(8,128)} %copy_subtract_fusion) | copy-start | bytes 2359300
  236.8 67.8 %all-gather.12.cloned.1.call-start = ((), (), s32[]{:S(2)}) async-start(), calls=%async_computation.6 | async-start | bytes 3932160 | tf_op jit(solution)/shard_map/all_gather | solution.py:157
  275.9 103.6 %all-reduce.17.cloned.1.call-start = ((), (), s32[]{:S(2)}) async-start(), calls=%async_computation.7 | async-start | bytes 131072 | tf_op jit(solution)/shard_map/psum | solution.py:160
  304.6 6.6 %copy-start = (f32[128,3,2,1024]{3,0,2,1:T(8,128)S(1)}, f32[128,3,2,1024]{3,0,2,1:T(8,128)}, u32[]{:S(2)}) copy-start(f32[128,3,2,1024]{3,0,2,1:T(8,128)} %all-gather.12.cloned.1.call-done) | copy-start | bytes 9437188
  310.9 265.7 %all-reduce.19.cloned.1.call-start = ((), (), s32[]{:S(2)}) async-start(), calls=%async_computation.8 | async-start | bytes 786432 | tf_op jit(solution)/shard_map/psum | solution.py:181
  409.1 8.1 %copy-start.14 = (s32[2,1024]{1,0:T(2,128)S(1)}, s32[2,1024]{1,0:T(2,128)}, u32[]{:S(2)}) copy-start(s32[2,1024]{1,0:T(2,128)} %param.8) | copy-start | bytes 24580
  409.2 8.1 %copy-start.15 = (f32[8]{0:T(128)S(1)}, f32[8]{0:T(128)}, u32[]{:S(2)}) copy-start(f32[8]{0:T(128)} %param.9) | copy-start | bytes 100
  411.0 69.1 %collective-permute-start = (f32[128,3,1,1024]{3,0,2,1:T(8,128)}, f32[128,3,1,1024]{3,0,2,1:T(8,128)}, u32[]{:S(2)}, u32[]{:S(2)}) collective-permute-start(f32[128,3,1,1024]{3,0,2,1:T(8,128)} %get-tuple-element.29), channel_id=1, source_target_pairs={{0,4},{4,8},{8,12},{12,16},{16,20},{20,24},{24,28},{1,5},{5,9},{9,... | collective-permute-start | bytes 4718600 | tf_op jit(solution)/shard_map/ppermute | solution.py:22
  415.6 64.6 %collective-permute-start.1 = (f32[128,3,1,1024]{3,0,2,1:T(8,128)}, f32[128,3,1,1024]{3,0,2,1:T(8,128)}, u32[]{:S(2)}, u32[]{:S(2)}) collective-permute-start(f32[128,3,1,1024]{3,0,2,1:T(8,128)} %get-tuple-element.30), channel_id=1, source_target_pairs={{4,0},{8,4},{12,8},{16,12},{20,16},{24,20},{28,24},{5,1},{9,5},{13... | collective-permute-start | bytes 4718600 | tf_op jit(solution)/shard_map/ppermute | solution.py:23
  418.2 0.9 copy-start.1
  419.1 13.9 %slice-start = ((s8[6291456]{0:T(1024)(128)(4,1)}), s8[4194304]{0:T(1024)(128)(4,1)S(1)}, s32[]{:S(2)}) async-start(s8[6291456]{0:T(1024)(128)(4,1)} %bitcast.118), calls=%async_computation.11 | async-start | bytes 8388608
  423.1 9.9 %slice-start.1 = ((s8[6291456]{0:T(1024)(128)(4,1)}), s8[2097152]{0:T(1024)(128)(4,1)S(1)}, s32[]{:S(2)}) async-start(s8[6291456]{0:T(1024)(128)(4,1)} %bitcast.118), calls=%async_computation.12 | async-start | bytes 4194304
  423.2 9.9 %copy-start.13 = (f32[3,2,1024]{2,1,0:T(2,128)S(1)}, f32[3,2,1024]{2,1,0:T(2,128)}, u32[]{:S(2)}) copy-start(f32[3,2,1024]{2,1,0:T(2,128)} %param.7) | copy-start | bytes 73732
  492.8 3.2 copy-start.6
  492.8 1.6 copy-start.8
  492.8 1.9 copy-start.11
  494.2 1.8 copy-start.4
  496.0 7.3 %copy-start.9 = (f32[128,1,2,1024]{3,0,2,1:T(8,128)}, f32[128,1,2,1024]{3,0,2,1:T(8,128)S(1)}, u32[]{:S(2)}) copy-start(f32[128,1,2,1024]{3,0,2,1:T(8,128)S(1)} %add_bitcast_fusion) | copy-start | bytes 3145732
  504.1 4.5 copy-start.2
  504.1 6.0 %copy-start.5 = (f32[128,1,2,1024]{3,0,2,1:T(8,128)S(1)}, f32[128,1,2,1024]{3,0,2,1:T(8,128)}, u32[]{:S(2)}) copy-start(f32[128,1,2,1024]{3,0,2,1:T(8,128)} %copy-done.4) | copy-start | bytes 3145732
  504.1 6.0 %copy-start.7 = (f32[128,1,2,1024]{3,0,2,1:T(8,128)S(1)}, f32[128,1,2,1024]{3,0,2,1:T(8,128)}, u32[]{:S(2)}) copy-start(f32[128,1,2,1024]{3,0,2,1:T(8,128)} %copy-done.6) | copy-start | bytes 3145732
  504.1 6.0 %copy-start.10 = (f32[128,1,2,1024]{3,0,2,1:T(8,128)S(1)}, f32[128,1,2,1024]{3,0,2,1:T(8,128)}, u32[]{:S(2)}) copy-start(f32[128,1,2,1024]{3,0,2,1:T(8,128)} %copy-done.9) | copy-start | bytes 3145732
Sparse Core Ops, SparseCore 0:
  10.1 31.2 all-gather.7
  52.3 40.2 all-gather.13
  105.2 36.7 reduce-scatter.2
  144.4 28.5 all-gather.9
  184.5 39.5 all-gather.15
  236.9 36.8 reduce-scatter.4
  276.0 28.5 all-gather.11
  311.0 68.4 all-reduce.16
  504.2 72.4 all-reduce.18
